TPU v7x, 32 devices: a whole 2x2x4 slice. The times are simulated.
32 devices in a mesh: row: 16 (over z, y, x), col: 2 (over core).
Axes of the slice: x: 2, y: 2, z: 4, core: 2. Of those that a mesh axis runs over, the one named last changes fastest.
Arguments:
- eigenvectors: float32 [2, 20480, 1024], P(None, 'row', 'col'), may hold values from -6 to 6
- reflectors: float32 [4, 2, 20480, 128], P(None, None, 'row', 'col'), may hold values from -0.03125 to 0.03125
- reflector_factors: float32 [4, 2, 128, 128], replicated, as said below
Outputs:
- transformed: float32 [2, 20480, 1024], P(None, 'row', 'col')
Inputs may be any that keep to these rules, and one draw needn't show every extreme that they name: Each block of reflector_factors is upper triangular in both parts; the real part of its diagonal lies between 1 and 2.
All inputs are finite; a program needn't handle non-finite values.
Results may differ from a plain program's by a relative error of at most 0.00017.
Values sent between devices are 32-bit elements; how exact they have to be, the bound alone decides.
A program may use at most 128 MiB of HBM per device.

v0:
```python
import jax
import jax.numpy as jnp
from jax import lax
from jax.sharding import PartitionSpec as P


def complex_product(left_side, right_side):
    real_part = jnp.dot(left_side[0], right_side[0], precision=lax.Precision.HIGHEST) - jnp.dot(
        left_side[1], right_side[1], precision=lax.Precision.HIGHEST
    )
    imag_part = jnp.dot(left_side[0], right_side[1], precision=lax.Precision.HIGHEST) + jnp.dot(
        left_side[1], right_side[0], precision=lax.Precision.HIGHEST
    )
    return jnp.stack([real_part, imag_part])


def adjoint_product(left_side, right_side):
    real_part = jnp.dot(left_side[0].T, right_side[0], precision=lax.Precision.HIGHEST) + jnp.dot(
        left_side[1].T, right_side[1], precision=lax.Precision.HIGHEST
    )
    imag_part = jnp.dot(left_side[0].T, right_side[1], precision=lax.Precision.HIGHEST) - jnp.dot(
        left_side[1].T, right_side[0], precision=lax.Precision.HIGHEST
    )
    return jnp.stack([real_part, imag_part])


def shards(eigenvectors, reflectors, reflector_factors):
    current = eigenvectors
    block_count = reflectors.shape[0]
    for block_index in reversed(range(block_count)):
        vectors = lax.all_gather(reflectors[block_index], "col", axis=2, tiled=True)
        result = complex_product(
            reflector_factors[block_index], lax.psum(adjoint_product(vectors, current), "row")
        )
        current = current - complex_product(vectors, result)
    return current


def solution(mesh):
    placed = (P(None, "row", "col"), P(None, None, "row", "col"), P())
    return jax.shard_map(
        shards, mesh=mesh, in_specs=placed, out_specs=P(None, "row", "col"), check_vma=False
    )
```

profile of v0, /device:TPU:0, one launch (start us, length us, event | category | flops | bytes accessed | tf_op | source)
XLA Modules:
  0.0 599.7 jit_solution(16532842886531282741)
XLA Ops:
  6.5 3.2 fusion.104
  9.8 12.2 %all-gather.9.cloned.1.call-done = f32[1,2,1280,128]{2,3,1,0:T(8,128)} async-done(((f32[1,2,1280,64]{2,3,1,0:T(8,128)}), f32[1,2,1280,128]{2,3,1,0:T(8,128)}) %all-gather.9.cloned.1.call-update) | async-done | bytes 1310736 | tf_op jit(solution)/shard_map/all_gather | solution.py:31
  22.1 3.7 fusion.8
  25.7 3.6 fusion.10
  34.2 6.4 %copy.4 = f32[2,1280,512]{1,2,0:T(8,128)} copy(f32[2,1280,512]{2,1,0:T(8,128)} %param.3) | data formatting | bytes 10485760 | tf_op args[0]
  40.6 102.5 %all-reduce.5.cloned.1.call-done = f32[2,128,512]{2,1,0:T(8,128)} async-done(((f32[2,128,512]{2,1,0:T(8,128)}), f32[2,128,512]{2,1,0:T(8,128)}) %all-reduce.5.cloned.1.call-update) | async-done | bytes 524304 | tf_op jit(solution)/shard_map/psum | solution.py:33
  151.5 2.3 fusion.56
  153.8 2.3 fusion
  156.2 2.3 fusion.1
  160.0 3.2 maximum_subtract_fusion
  163.2 4.2 fusion.16
  167.4 4.2 fusion.17
  177.8 106.6 %all-reduce.7.cloned.1.call-done = f32[2,128,512]{1,2,0:T(8,128)} async-done(((f32[2,128,512]{1,2,0:T(8,128)}), f32[2,128,512]{1,2,0:T(8,128)}) %all-reduce.7.cloned.1.call-update) | async-done | bytes 524304 | tf_op jit(solution)/shard_map/psum | solution.py:33
  289.8 2.3 fusion.59
  292.1 2.3 fusion.58
  294.3 2.3 fusion.2
  296.7 2.3 fusion.3
  300.6 3.2 maximum_subtract_fusion.1
  303.8 4.2 fusion.20
  308.0 4.2 fusion.21
  318.5 106.5 %all-reduce.9.cloned.1.call-done = f32[2,128,512]{1,2,0:T(8,128)} async-done(((f32[2,128,512]{1,2,0:T(8,128)}), f32[2,128,512]{1,2,0:T(8,128)}) %all-reduce.9.cloned.1.call-update) | async-done | bytes 524304 | tf_op jit(solution)/shard_map/psum | solution.py:33
  432.7 2.3 fusion.60
  435.0 2.3 fusion.4
  437.3 2.4 fusion.5
  441.2 3.2 maximum_subtract_fusion.2
  444.4 4.2 fusion.24
  448.6 4.2 fusion.25
  458.2 107.4 %all-reduce.11.cloned.1.call-done = f32[2,128,512]{1,2,0:T(8,128)} async-done(((f32[2,128,512]{1,2,0:T(8,128)}), f32[2,128,512]{1,2,0:T(8,128)}) %all-reduce.11.cloned.1.call-update) | async-done | bytes 524304 | tf_op jit(solution)/shard_map/psum | solution.py:33
  571.0 2.5 fusion.63
  578.1 3.9 fusion.7
  582.0 4.5 maximum_subtract_fusion.3
  586.5 5.9 copy.5
  (125 shorter events, 58.5 us)
Async XLA Ops:
  6.5 15.5 %all-gather.9.cloned.1.call-start = ((), (), s32[]{:S(2)}) async-start(), calls=%async_computation.4 | async-start | bytes 1966080 | tf_op jit(solution)/shard_map/all_gather | solution.py:31
  9.8 133.3 %all-reduce.5.cloned.1.call-start = ((), (), s32[]{:S(2)}) async-start(), calls=%async_computation | async-start | bytes 1048576 | tf_op jit(solution)/shard_map/psum | solution.py:33
  22.1 7.3 %copy-start.5 = (f32[2,1280,512]{2,1,0:T(8,128)S(1)}, f32[2,1280,512]{2,1,0:T(8,128)}, u32[]{:S(2)}) copy-start(f32[2,1280,512]{2,1,0:T(8,128)} %param.3) | copy-start | bytes 15728644
  33.4 129.7 %all-gather.11.cloned.1.call-start = ((), (), s32[]{:S(2)}) async-start(), calls=%async_computation.5 | async-start | bytes 1966080 | tf_op jit(solution)/shard_map/all_gather | solution.py:31
  34.2 108.9 %copy-start.26 = (f32[4,2,128,128]{3,2,1,0:T(8,128)S(1)}, f32[4,2,128,128]{3,2,1,0:T(8,128)}, u32[]{:S(2)}) copy-start(f32[4,2,128,128]{3,2,1,0:T(8,128)} %param.5) | copy-start | bytes 1572868
  34.2 250.2 %all-reduce.7.cloned.1.call-start = ((), (), s32[]{:S(2)}) async-start(), calls=%async_computation.1 | async-start | bytes 1048576 | tf_op jit(solution)/shard_map/psum | solution.py:33
  149.3 4.5 copy-start.25
  151.5 8.4 %slice-start = ((s8[5242880]{0:T(1024)(128)(4,1)}), s8[4194304]{0:T(1024)(128)(4,1)S(1)}, s32[]{:S(2)}) async-start(s8[5242880]{0:T(1024)(128)(4,1)} %bitcast.262), calls=%async_computation.8 | async-start | bytes 8388608
  153.8 6.1 %slice-start.1 = ((s8[5242880]{0:T(1024)(128)(4,1)}), s8[1048576]{0:T(1024)(128)(4,1)S(1)}, s32[]{:S(2)}) async-start(s8[5242880]{0:T(1024)(128)(4,1)} %bitcast.262), calls=%async_computation.9 | async-start | bytes 2097152
  163.2 8.4 %copy-start.6 = (f32[2,1280,512]{1,2,0:T(8,128)S(1)}, f32[2,1280,512]{1,2,0:T(8,128)}, u32[]{:S(2)}) copy-start(f32[2,1280,512]{1,2,0:T(8,128)} %maximum_subtract_fusion) | copy-start | bytes 15728644
  167.4 4.2 copy-start.18
  176.9 126.9 %all-gather.13.cloned.1.call-start = ((), (), s32[]{:S(2)}) async-start(), calls=%async_computation.6 | async-start | bytes 1966080 | tf_op jit(solution)/shard_map/all_gather | solution.py:31
  177.5 247.5 %all-reduce.9.cloned.1.call-start = ((), (), s32[]{:S(2)}) async-start(), calls=%async_computation.2 | async-start | bytes 1048576 | tf_op jit(solution)/shard_map/psum | solution.py:33
  284.3 5.5 copy-start.19
  292.1 8.5 %slice-start.2 = ((s8[5242880]{0:T(1024)(128)(4,1)}), s8[4194304]{0:T(1024)(128)(4,1)S(1)}, s32[]{:S(2)}) async-start(s8[5242880]{0:T(1024)(128)(4,1)} %bitcast.264), calls=%async_computation.10 | async-start | bytes 8388608
  294.3 6.2 %slice-start.3 = ((s8[5242880]{0:T(1024)(128)(4,1)}), s8[1048576]{0:T(1024)(128)(4,1)S(1)}, s32[]{:S(2)}) async-start(s8[5242880]{0:T(1024)(128)(4,1)} %bitcast.264), calls=%async_computation.11 | async-start | bytes 2097152
  303.8 8.4 %copy-start.4 = (f32[2,1280,512]{1,2,0:T(8,128)S(1)}, f32[2,1280,512]{1,2,0:T(8,128)}, u32[]{:S(2)}) copy-start(f32[2,1280,512]{1,2,0:T(8,128)} %maximum_subtract_fusion.1) | copy-start | bytes 15728644
  308.0 4.2 copy-start.20
  317.5 126.9 %all-gather.15.cloned.1.call-start = ((), (), s32[]{:S(2)}) async-start(), calls=%async_computation.7 | async-start | bytes 1966080 | tf_op jit(solution)/shard_map/all_gather | solution.py:31
  318.3 247.3 %all-reduce.11.cloned.1.call-start = ((), (), s32[]{:S(2)}) async-start(), calls=%async_computation.3 | async-start | bytes 1048576 | tf_op jit(solution)/shard_map/psum | solution.py:33
  425.0 5.5 copy-start.21
  432.7 8.5 %slice-start.4 = ((s8[5242880]{0:T(1024)(128)(4,1)}), s8[4194304]{0:T(1024)(128)(4,1)S(1)}, s32[]{:S(2)}) async-start(s8[5242880]{0:T(1024)(128)(4,1)} %bitcast.266), calls=%async_computation.12 | async-start | bytes 8388608
  435.0 6.2 %slice-start.5 = ((s8[5242880]{0:T(1024)(128)(4,1)}), s8[1048576]{0:T(1024)(128)(4,1)S(1)}, s32[]{:S(2)}) async-start(s8[5242880]{0:T(1024)(128)(4,1)} %bitcast.266), calls=%async_computation.13 | async-start | bytes 2097152
  435.0 6.2 %copy-start.12 = (f32[1,1280,512]{1,2,0:T(8,128)S(1)}, f32[1,1280,512]{1,2,0:T(8,128)}, u32[]{:S(2)}) copy-start(f32[1,1280,512]{1,2,0:T(8,128)} %copy-done.11) | copy-start | bytes 7864324
  444.4 8.4 %copy-start.7 = (f32[2,1280,512]{1,2,0:T(8,128)S(1)}, f32[2,1280,512]{1,2,0:T(8,128)}, u32[]{:S(2)}) copy-start(f32[2,1280,512]{1,2,0:T(8,128)} %maximum_subtract_fusion.2) | copy-start | bytes 15728644
  448.6 4.2 copy-start.22
  565.6 5.5 copy-start.23
  571.0 10.9 %copy-start.17 = (f32[1,1280,512]{1,2,0:T(8,128)S(1)}, f32[1,1280,512]{1,2,0:T(8,128)}, u32[]{:S(2)}) copy-start(f32[1,1280,512]{1,2,0:T(8,128)} %copy-done.16) | copy-start | bytes 7864324
  573.5 8.4 %slice-start.6 = ((s8[5242880]{0:T(1024)(128)(4,1)}), s8[4194304]{0:T(1024)(128)(4,1)S(1)}, s32[]{:S(2)}) async-start(s8[5242880]{0:T(1024)(128)(4,1)} %bitcast.268), calls=%async_computation.14 | async-start | bytes 8388608
  575.8 6.1 %slice-start.7 = ((s8[5242880]{0:T(1024)(128)(4,1)}), s8[1048576]{0:T(1024)(128)(4,1)S(1)}, s32[]{:S(2)}) async-start(s8[5242880]{0:T(1024)(128)(4,1)} %bitcast.268), calls=%async_computation.15 | async-start | bytes 2097152
  575.8 6.1 %copy-start.13 = (f32[1,1280,512]{1,2,0:T(8,128)S(1)}, f32[1,1280,512]{1,2,0:T(8,128)}, u32[]{:S(2)}) copy-start(f32[1,1280,512]{1,2,0:T(8,128)} %copy-done.11) | copy-start | bytes 7864324
  575.8 6.1 %copy-start.15 = (f32[1,1280,512]{1,2,0:T(8,128)S(1)}, f32[1,1280,512]{1,2,0:T(8,128)}, u32[]{:S(2)}) copy-start(f32[1,1280,512]{1,2,0:T(8,128)} %copy-done.14) | copy-start | bytes 7864324
  (11 other events, 32.3 us)
Sparse Core Ops, SparseCore 0:
  9.9 12.1 all-gather.8
  33.5 109.4 all-reduce.4
  144.7 8.3 all-gather.10
  177.0 107.2 all-reduce.6
  285.7 8.3 all-gather.12
  317.6 107.2 all-reduce.8
  426.6 8.3 all-gather.14
  458.3 107.2 all-reduce.10
where the time goes:
time: 605 us; the launch traced here: 600 us
  waiting for transfers between devices  437 us (72%)
  matrix products  110 us (18%)
  local copies, waits for them, and re-layouts  20.1 us (3%)
  other arithmetic  17.5 us (3%)
  between operations  14.7 us (2%)
    psum x4, waiting for transfers between devices, shards(): lax.psum(adjoint_product(vectors, current), 'row')  423 us
    dot_general x8, matrix products, complex_product(): jnp.dot(left_side[1], right_side[0], precision=lax.Precision.HIGHEST)  16.4 us
    dot_general x8, matrix products, complex_product(): jnp.dot(left_side[0], right_side[1], precision=lax.Precision.HIGHEST)  14.9 us
    dot_general x8, matrix products, complex_product(): jnp.dot(left_side[0], right_side[0], precision=lax.Precision.HIGHEST)  14.8 us
    dot_general x8, matrix products, complex_product(): jnp.dot(left_side[1], right_side[1], precision=lax.Precision.HIGHEST)  14.7 us
    dot_general x4, matrix products, adjoint_product(): jnp.dot(left_side[1].T, right_side[0], precision=lax.Precision.HIGHEST)  14.3 us
    dot_general x4, matrix products, adjoint_product(): jnp.dot(left_side[0].T, right_side[0], precision=lax.Precision.HIGHEST)  14.1 us
    sub x4, other arithmetic, shards(): current = current - complex_product(vectors, result)  14.1 us
  transfers between devices with their start and end apart: 8, of which 5 were waited for; matrix products, arithmetic and copies ran while one was open for 10% of the time, Pallas kernels for 0%

commit v1 on v0

v1 whole, which is shorter than its diff:
```python
import jax
import jax.numpy as jnp
from jax import lax
from jax.sharding import PartitionSpec as P


def product(spec, left_side, right_side):
    return jnp.einsum(spec, left_side, right_side, precision=lax.Precision.HIGH)


def adjoint_transposed(columns, vectors):
    spec = "nm,...nk->...mk"
    real_part = product(spec, columns[0], vectors[..., 0, :, :]) + product(spec, columns[1], vectors[..., 1, :, :])
    imag_part = product(spec, columns[1], vectors[..., 0, :, :]) - product(spec, columns[0], vectors[..., 1, :, :])
    return jnp.stack([real_part, imag_part], axis=-3)


def complex_rows(spec, left_side, right_side):
    real_part = product(spec, left_side[0], right_side[0]) - product(spec, left_side[1], right_side[1])
    imag_part = product(spec, left_side[0], right_side[1]) + product(spec, left_side[1], right_side[0])
    return jnp.stack([real_part, imag_part])


def merged_shards(eigenvectors, reflectors, reflector_factors):
    block_count, _, rows, share = reflectors.shape
    vectors = lax.all_gather(reflectors, "col", axis=3, tiled=True)
    width = vectors.shape[3]
    grams = []
    for block in range(block_count - 1):
        later = jnp.concatenate([reflectors[c] for c in range(block + 1, block_count)], axis=2)
        grams.append(adjoint_transposed(later, vectors[block]))
    gram = lax.psum(jnp.concatenate(grams, axis=1), "row")
    gram = gram.reshape(2, -1, share, width)
    gram = lax.all_gather(gram, "col", axis=2, tiled=True)
    projected = lax.psum_scatter(
        adjoint_transposed(eigenvectors, vectors), "row", scatter_dimension=2, tiled=True
    )
    results = [None] * block_count
    for block in reversed(range(block_count)):
        start = sum(block_count - 1 - b for b in range(block))
        sums = projected[block]
        for c in range(block + 1, block_count):
            sums = sums - complex_rows("mk,kj->mj", results[c], gram[:, start + c - block - 1])
        results[block] = complex_rows("mk,jk->mj", sums, reflector_factors[block])
    result = lax.all_gather(jnp.concatenate(results, axis=2), "row", axis=1, tiled=True)
    flat = vectors.transpose(1, 2, 0, 3).reshape(2, rows, block_count * width)
    return eigenvectors - complex_rows("nk,mk->nm", flat, result)


def solution(mesh):
    placed = (P(None, "row", "col"), P(None, None, "row", "col"), P())
    return jax.shard_map(
        merged_shards, mesh=mesh, in_specs=placed, out_specs=P(None, "row", "col"), check_vma=False
    )
```

time: 605 us -> 295 us (0.49)
  waiting for transfers between devices: 437 us -> 199 us
  matrix products: 110 us -> 44 us
  other arithmetic: 17.5 us -> 7.6 us
  local copies, waits for them, and re-layouts: 20.1 us -> 27.4 us
    psum x4 -> x0, waiting for transfers between devices: 423 us -> none  [shards(): lax.psum(adjoint_product(vectors, current), 'row')]
    unnamed x8 -> x4, waiting for transfers between devices: 1.99 us -> 134 us
    dot_general x48 -> x60, matrix products: 110 us -> 44 us  [product(): return jnp.einsum(spec, left_side, right_side, precision=lax.Precision.HIGH)]
    all_gather x4 -> x2, waiting for transfers between devices: 12.2 us -> 64.8 us  [the longest x1 49.9 us: merged_shards(): lax.all_gather(jnp.concatenate(results, axis=2), 'row', axis=1, tiled=True)]
    sub x4, other arithmetic: 14.1 us -> 3.09 us  [the longest x1 2.96 us: merged_shards(): return eigenvectors - complex_rows('nk,mk->nm', flat, result)]
  transfers between devices with their start and end apart: 8 -> 3, of which waited for: 5 -> 3; matrix products, arithmetic and copies ran while one was open for 10% -> 5% of each run, Pallas kernels for 0% -> 0%
where the time goes in v1:
time: 295 us; the launch traced here: 294 us
  waiting for transfers between devices  199 us (67%)
  matrix products  44 us (15%)
  local copies, waits for them, and re-layouts  27.4 us (9%)
  between operations  14.2 us (5%)
  other arithmetic  7.6 us (3%)
    unnamed x4, waiting for transfers between devices  134 us
    all_gather x1, waiting for transfers between devices, merged_shards(): lax.all_gather(jnp.concatenate(results, axis=2), 'row', axis=1, tiled=True)  49.9 us
    dot_general x60, matrix products, product(): return jnp.einsum(spec, left_side, right_side, precision=lax.Precision.HIGH)  44 us
    all_gather x1, waiting for transfers between devices, merged_shards(): vectors = lax.all_gather(reflectors, 'col', axis=3, tiled=True)  14.9 us
    unnamed x27, local copies, waits for them, and re-layouts  10.3 us
  transfers between devices with their start and end apart: 3, of which 3 were waited for; matrix products, arithmetic and copies ran while one was open for 5% of the time, Pallas kernels for 0%

profile of v1, /device:TPU:0, one launch (start us, length us, event | category | flops | bytes accessed | tf_op | source)
XLA Modules:
  0.0 294.5 jit_solution(11626440133029027838)
XLA Ops:
  6.5 3.4 %copy.41 = f32[4,2,1280,64]{2,3,0,1:T(8,128)} copy(f32[4,2,1280,64]{2,3,1,0:T(8,128)} %param.4) | data formatting | bytes 5242880 | tf_op args[1]
  10.0 1.6 slice_bitcast_fusion.34
  11.7 1.5 pad_maximum_fusion.1
  13.2 14.9 %all-gather.3.cloned.1.call-done = f32[4,2,1280,128]{2,3,0,1:T(8,128)} async-done(((f32[4,2,1280,64]{2,3,0,1:T(8,128)}), f32[4,2,1280,128]{2,3,0,1:T(8,128)}) %all-gather.3.cloned.1.call-update) | async-done | bytes 5242896 | tf_op jit(solution)/shard_map/all_gather | solution.py:26
  28.1 4.9 %fusion.4 = f32[4,128,512]{2,1,0:T(8,128)S(1)} fusion(f32[4,2,1280,128]{2,3,0,1:T(8,128)} %all-gather.3.cloned.1.call-done, f32[2,1280,512]{2,1,0:T(8,128)} %param.3), kind=kOutput, calls=%fused_computation.9 | convolution fusion | flops 2013265920 | bytes 6291456 | tf_op jit(solution)/shard_map/nm,...nk->...mk/dot_general | solution.py:8
  33.0 4.2 %fusion.2 = f32[4,128,512]{2,1,0:T(8,128)S(1)} fusion(f32[4,2,1280,128]{2,3,0,1:T(8,128)S(1)} %copy-done, f32[2,1280,512]{2,1,0:T(8,128)} %param.3), kind=kOutput, calls=%fused_computation.7 | convolution fusion | flops 2013265920 | bytes 6291456 | tf_op jit(solution)/shard_map/nm,...nk->...mk/dot_general | solution.py:8
  37.2 2.4 fusion.17
  39.6 2.4 fusion.23
  42.0 1.5 pad_maximum_fusion
  43.5 2.9 copy.42
  46.4 2.1 fusion.49
  48.5 2.1 fusion.48
  50.6 1.7 fusion.53
  52.3 1.5 fusion.54
  53.8 1.6 fusion.55
  56.5 0.6 fusion.27
  58.9 0.8 maximum_maximum_fusion
  59.8 0.7 dynamic-slice
  61.2 133.8 %all-reduce.4.cloned.1.call-done = (f32[4,2,512,128]{3,0,1,2:T(4,128)}, f32[2,6,64,128]{3,2,1,0:T(8,128)}) async-done(((f32[4,2,512,128]{3,0,1,2:T(4,128)}, f32[2,6,64,128]{3,2,1,0:T(8,128)}), (f32[4,2,512,128]{3,0,1,2:T(4,128)}, f32[2,6,64,128]{3,2,1,0:T(8,128)})) %all-reduce.4.cloned.1.call-update) | async-done | bytes 2490384
  194.9 0.9 constant_dynamic-slice_fusion.4
  196.2 2.6 all_gather.10
  200.1 1.2 constant_dynamic-slice_fusion.3
  206.5 0.7 maximum_maximum_fusion.1
  207.2 6.1 %copy.47 = f32[2,1280,512]{1,2,0:T(8,128)} copy(f32[2,1280,512]{2,1,0:T(8,128)} %param.3) | data formatting | bytes 10485760 | tf_op args[0]
  213.3 4.6 %fusion.127 = (f32[1,1280,4,128]{1,3,2,0:T(8,128)}, f32[1,1280,4,128]{1,3,2,0:T(8,128)S(1)}) fusion(f32[2,1280,4,128]{1,3,2,0:T(8,128)} %bitcast.315), kind=kLoop, calls=%fused_computation.193 | loop fusion | bytes 10485760 | tf_op jit(solution)/shard_map/slice | solution.py:19
  217.9 49.9 %all-gather.5.cloned.1.call-done = f32[2,512,512]{2,1,0:T(8,128)} async-done(((f32[2,32,512]{2,1,0:T(8,128)}), f32[2,512,512]{2,1,0:T(8,128)}) %all-gather.5.cloned.1.call-update) | async-done | bytes 2097168 | tf_op jit(solution)/shard_map/all_gather | solution.py:45
  267.8 3.8 %fusion.46 = f32[512,1280]{1,0:T(8,128)S(1)} fusion(f32[1280,512]{0,1:T(8,128)S(1)} %bitcast.318, f32[2,512,512]{2,1,0:T(8,128)} %all-gather.5.cloned.1.call-done), kind=kOutput, calls=%fused_computation.75 | convolution fusion | flops 2013265920 | bytes 6291456 | tf_op jit(solution)/shard_map/nk,mk->nm/dot_general | solution.py:8
  271.6 2.4 fusion.47
  274.0 2.5 fusion
  276.6 2.5 fusion.1
  279.1 3.0 %maximum_subtract_fusion = f32[2,1280,512]{1,2,0:T(8,128)} fusion(f32[2,1280,512]{1,2,0:T(8,128)S(1)} %bitcast.323, f32[1,1280,512]{1,2,0:T(8,128)S(1)} %fusion.1, f32[1,1280,512]{1,2,0:T(8,128)S(1)} %fusion), kind=kLoop, calls=%fused_computation | loop fusion | flops 2621440 | bytes 15728640 | tf_op jit(solution)/shard_map/sub | solution.py:47
  282.1 5.9 %copy.48 = f32[2,1280,512]{2,1,0:T(8,128)} copy(f32[2,1280,512]{1,2,0:T(8,128)} %maximum_subtract_fusion) | data formatting | bytes 10485760 | tf_op jit(solution)/shard_map/sub | solution.py:47
  (85 shorter events, 9.8 us)
Async XLA Ops:
  6.5 21.5 %all-gather.3.cloned.1.call-start = ((), (), s32[]{:S(2)}) async-start(), calls=%async_computation | async-start | bytes 7864320 | tf_op jit(solution)/shard_map/all_gather | solution.py:26
  10.0 184.9 %all-reduce.4.cloned.1.call-start = ((), (), s32[]{:S(2)}) async-start(), calls=%async_computation.2 | async-start | bytes 4980736
  28.1 4.9 %copy-start = (f32[4,2,1280,128]{2,3,0,1:T(8,128)S(1)}, f32[4,2,1280,128]{2,3,0,1:T(8,128)}, u32[]{:S(2)}) copy-start(f32[4,2,1280,128]{2,3,0,1:T(8,128)} %all-gather.3.cloned.1.call-done) | copy-start | bytes 15728644
  33.0 4.2 %copy-start.1 = (f32[2,1280,512]{2,1,0:T(8,128)S(1)}, f32[2,1280,512]{2,1,0:T(8,128)}, u32[]{:S(2)}) copy-start(f32[2,1280,512]{2,1,0:T(8,128)} %param.3) | copy-start | bytes 15728644
  42.0 13.4 %slice-start = ((s8[5242880]{0:T(1024)(128)(4,1)}), s8[1048576]{0:T(1024)(128)(4,1)S(1)}, s32[]{:S(2)}) async-start(s8[5242880]{0:T(1024)(128)(4,1)} %bitcast.316), calls=%async_computation.3 | async-start | bytes 2097152
  46.4 9.0 %slice-start.1 = ((s8[5242880]{0:T(1024)(128)(4,1)}), s8[4194304]{0:T(1024)(128)(4,1)S(1)}, s32[]{:S(2)}) async-start(s8[5242880]{0:T(1024)(128)(4,1)} %bitcast.316), calls=%async_computation.4 | async-start | bytes 8388608
  48.5 5.3 %copy-start.4 = (f32[4,2,1280,64]{2,3,1,0:T(8,128)S(1)}, f32[4,2,1280,64]{2,3,1,0:T(8,128)}, u32[]{:S(2)}) copy-start(f32[4,2,1280,64]{2,3,1,0:T(8,128)} %param.4) | copy-start | bytes 7864324
  50.6 5.3 %copy-start.3 = (f32[2,1280,192]{1,2,0:T(8,128)S(1)}, f32[2,1280,192]{1,2,0:T(8,128)}, u32[]{:S(2)}) copy-start(f32[2,1280,192]{1,2,0:T(8,128)} %pad_maximum_fusion.1) | copy-start | bytes 5898244
  58.0 1.8 copy-start.7
  58.0 137.8 %copy-start.6 = (f32[4,2,128,128]{3,2,1,0:T(8,128)S(1)}, f32[4,2,128,128]{3,2,1,0:T(8,128)}, u32[]{:S(2)}) copy-start(f32[4,2,128,128]{3,2,1,0:T(8,128)} %param.5) | copy-start | bytes 1572868
  59.7 208.0 %all-gather.5.cloned.1.call-start = ((), (), s32[]{:S(2)}) async-start(), calls=%async_computation.1 | async-start | bytes 2228224 | tf_op jit(solution)/shard_map/all_gather | solution.py:45
  267.8 3.8 %copy-start.5 = (f32[2,512,512]{2,1,0:T(8,128)S(1)}, f32[2,512,512]{2,1,0:T(8,128)}, u32[]{:S(2)}) copy-start(f32[2,512,512]{2,1,0:T(8,128)} %all-gather.5.cloned.1.call-done) | copy-start | bytes 6291460
  271.6 2.4 copy-start.2
  274.0 5.1 %slice-start.2 = ((s8[5242880]{0:T(1024)(128)(4,1)}), s8[4194304]{0:T(1024)(128)(4,1)S(1)}, s32[]{:S(2)}) async-start(s8[5242880]{0:T(1024)(128)(4,1)} %bitcast.322), calls=%async_computation.5 | async-start | bytes 8388608
  276.6 2.5 slice-start.3
Sparse Core Ops, SparseCore 0:
  10.1 17.9 all-gather.2
  59.9 135.0 all-reduce.3
  207.3 60.4 all-gather.4

commit v2 on v1

--- a/solution.py
+++ b/solution.py
@@ -1,7 +1,357 @@
 import jax
 import jax.numpy as jnp
 from jax import lax
+from jax.experimental import pallas as pl
+from jax.experimental.pallas import tpu as pltpu
 from jax.sharding import PartitionSpec as P
+
+F32 = jnp.float32
+BF16 = jnp.bfloat16
+BITS = 4
+GRAM = 4
+ORDERS = {3: (0, 1, 2, 3), 2: (1, 2, 0, 3), GRAM: (1, 0, 2, 3), 1: (2, 0, 1, 3), 0: (0, 1, 2, 3)}
+
+
+def split(value):
+    high = value.astype(BF16)
+    return high, (value - high.astype(F32)).astype(BF16)
+
+
+def dot(left, right):
+    return jnp.dot(left, right, preferred_element_type=F32)
+
+
+def dot_lanes(left, right):
+    return lax.dot_general(left, right, (((1,), (1,)), ((), ())), preferred_element_type=F32)
+
+
+def kernel(z_hbm, v_hbm, factors, out_hbm, z, zt, w_own, w_other, vt, forms, acc, gacc,
+           slots, gslots, xt, gx, gother, xk, gram, z_sem, v_sem, out_sem, pair_send, pair_recv,
+           row_send, row_recv):
+    rows, columns = z.shape[1], z.shape[2]
+    blocks = w_own.shape[0]
+    share = w_own.shape[2] // 2
+    row, col = lax.axis_index("row"), lax.axis_index("col")
+    mine = [lax.rem(row // (1 << bit), 2) for bit in range(BITS)]
+    partner = [row + (1 << bit) * (1 - 2 * mine[bit]) for bit in range(BITS)]
+    sibling = {"row": row, "col": 1 - col}
+
+    z_in = [pltpu.make_async_copy(z_hbm.at[p], z.at[p], z_sem.at[p]) for p in range(2)]
+    v_in = [pltpu.make_async_copy(v_hbm.at[b], w_own.at[b], v_sem.at[b]) for b in range(blocks)]
+    for b in reversed(range(blocks)):
+        v_in[b].start()
+    for copy in z_in:
+        copy.start()
+
+    barrier = pltpu.get_barrier_semaphore()
+    for bit in range(BITS):
+        pl.semaphore_signal(barrier, inc=1, device_id={"row": partner[bit], "col": col},
+                            device_id_type=pl.DeviceIdType.MESH)
+    pl.semaphore_signal(barrier, inc=1, device_id=sibling, device_id_type=pl.DeviceIdType.MESH)
+    pl.semaphore_wait(barrier, BITS + 1)
+
+    sends = []
+
+    def send(source, target, send_sem, recv_sem, device):
+        copy = pltpu.make_async_remote_copy(
+            src_ref=source, dst_ref=target, send_sem=send_sem, recv_sem=recv_sem,
+            device_id=device, device_id_type=pl.DeviceIdType.MESH)
+        copy.start()
+        sends.append(copy)
+        return copy
+
+    v_copies = {}
+    for b in reversed(range(blocks)):
+        v_in[b].wait()
+        v_copies[b] = send(w_own.at[b], w_other.at[b], pair_send.at[b], pair_recv.at[b], sibling)
+
+    @pl.loop(0, rows // 128)
+    def _(step):
+        part = pl.ds(pl.multiple_of(step * 128, 128), 128)
+        for b in range(blocks):
+            high, low = split(w_own[b, part, :].T)
+            for p in range(2):
+                vt[0, p, b * share:(b + 1) * share, part] = high[p * share:(p + 1) * share]
+                vt[1, p, b * share:(b + 1) * share, part] = low[p * share:(p + 1) * share]
+
+    for copy in z_in:
+        copy.wait()
+
+    @pl.loop(0, rows // 128)
+    def _(step):
+        part = pl.ds(pl.multiple_of(step * 128, 128), 128)
+        for p in range(2):
+            high, low = split(z[p, part, :].T)
+            zt[0, p, :, part] = high
+            zt[1, p, :, part] = low
+
+    lane = lax.broadcasted_iota(jnp.int32, (1, 128), 1)
+    sign = jnp.where(lane < share, 1.0, -1.0).astype(F32)
+
+    def make_forms(b):
+        v_copies[b].wait_recv()
+
+        @pl.loop(0, rows // 256)
+        def _(step):
+            part = pl.ds(pl.multiple_of(step * 256, 256), 256)
+            own, other = w_own[b, part, :], w_other[b, part, :]
+            halves = (jnp.where(col == 0, own, other), jnp.where(col == 0, other, own))
+            for h in range(2):
+                lanes = slice(b * 256 + h * 128, b * 256 + h * 128 + 128)
+                for form, value in ((0, halves[h] * sign), (1, pltpu.roll(halves[h], share, 1))):
+                    high, low = split(value)
+                    forms[form, 0, part, lanes] = high
+                    forms[form, 1, part, lanes] = low
+
+    def products(turned, b, first, count):
+        def body(step, total):
+            part = pl.ds(pl.multiple_of(step * 256, 256), 256)
+            for p in range(2):
+                high = turned[0, p, first:first + count, part]
+                low = turned[1, p, first:first + count, part]
+                f_high = forms[p, 0, part, b * 256:(b + 1) * 256]
+                f_low = forms[p, 1, part, b * 256:(b + 1) * 256]
+                total = total + dot(high, f_high) + dot(high, f_low) + dot(low, f_high)
+            return total
+
+        return lax.fori_loop(0, rows // 256, body, jnp.zeros((count, 256), F32))
+
+    def place(ref, prefix, free, fixed):
+        at = list(prefix)
+        for bit in reversed(range(BITS)):
+            at.append(slice(None) if bit in free else fixed[bit])
+        return ref.at[tuple(at)]
+
+    def buffers(chunk):
+        if chunk == GRAM:
+            return gacc, (), gslots, (), gx
+        return acc, (chunk,), slots, (chunk,), xt
+
+    pending = {}
+
+    def start_reduce(chunk, step):
+        source, prefix, slot, slot_prefix, _ = buffers(chunk)
+        order = ORDERS[chunk]
+        fixed = dict(enumerate(mine))
+        fixed[order[step]] = 1 - mine[order[step]]
+        target = slot[step].at[slot_prefix] if slot_prefix else slot[step]
+        pending[chunk] = send(
+            place(source, prefix, order[step + 1:], fixed), target,
+            row_send.at[chunk, step], row_recv.at[chunk, step],
+            {"row": partner[order[step]], "col": col})
+
+    def finish_reduce(chunk, step):
+        source, prefix, slot, slot_prefix, _ = buffers(chunk)
+        order = ORDERS[chunk]
+        pending[chunk].wait_recv()
+        held = place(source, prefix, order[step + 1:], dict(enumerate(mine)))
+        arrived = slot[step].at[slot_prefix] if slot_prefix else slot[step]
+        held[...] = held[...] + arrived[...]
+
+    def start_spread(chunk, step):
+        _, prefix, _, _, target = buffers(chunk)
+        order = ORDERS[chunk][::-1]
+        part = place(target, prefix, order[:step], dict(enumerate(mine)))
+        pending[chunk] = send(
+            part, part, row_send.at[chunk, BITS + step], row_recv.at[chunk, BITS + step],
+            {"row": partner[order[step]], "col": col})
+
+    def own_part(ref, prefix):
+        return place(ref, prefix, (), dict(enumerate(mine)))
+
+    def finish_gram():
+        gram_copy.wait_recv()
+        start = 0
+        for b in range(blocks - 1):
+            for c in range(b + 1, blocks):
+                for group in range(share // 8):
+                    q = (start * share) // 8 + group
+                    owner, sub = q // 3, q % 3
+                    at = (owner // 8, (owner // 4) % 2, (owner // 2) % 2, owner % 2, sub)
+                    own, other = gx[at], gother[at]
+                    halves = (jnp.where(col == 0, own, other), jnp.where(col == 0, other, own))
+                    for h in range(2):
+                        base = h * 2 * share + group * 8
+                        gram[start, base:base + 8, :] = halves[h]
+                        turned = jnp.concatenate(
+                            [pltpu.roll(halves[h][:, k:k + 128], share, 1) * -sign for k in (0, 128)], axis=1)
+                        gram[start, base + share:base + share + 8, :] = turned
+                start += 1
+
+    def dot3(left, high, low):
+        l_high, l_low = split(left)
+        return dot(l_high, high) + dot(l_high, low) + dot(l_low, high)
+
+    solved = {}
+
+    def solve(b):
+        sums = own_part(acc, (b,))[...]
+        start = sum(blocks - 1 - k for k in range(b))
+        for c in range(b + 1, blocks):
+            high, low = split(gram[start + c - b - 1])
+            sums = sums - dot3(solved[c], high, low)
+        high, low = split(factors[b])
+        solved[b] = dot3(sums, high, low)
+        own_part(xt, (b,))[...] = solved[b]
+
+    stage = {}
+
+    def advance(chunk):
+        nonlocal gram_copy
+        step = stage[chunk]
+        if step < BITS:
+            finish_reduce(chunk, step)
+            if step + 1 < BITS:
+                start_reduce(chunk, step + 1)
+            elif chunk == GRAM:
+                own_part(gx, ())[...] = own_part(gacc, ())[...]
+                start_spread(chunk, 0)
+            elif chunk == blocks - 1:
+                solve(chunk)
+                start_spread(chunk, 0)
+        elif step < 2 * BITS:
+            pending[chunk].wait_recv()
+            if step + 1 < 2 * BITS:
+                start_spread(chunk, step + 1 - BITS)
+            elif chunk == GRAM:
+                gram_copy = send(gx, gother, pair_send.at[GRAM], pair_recv.at[GRAM], sibling)
+        stage[chunk] += 1
+
+    gram_copy = None
+
+    def begin(chunk):
+        if chunk == GRAM:
+            q = 0
+            for b in range(blocks - 1):
+                count = share * (blocks - 1 - b)
+                value = products(vt, b, share * (b + 1), count)
+                for group in range(count // 8):
+                    owner, sub = q // 3, q % 3
+                    gacc[owner // 8, (owner // 4) % 2, (owner // 2) % 2, owner % 2, sub] = (
+                        value[group * 8:group * 8 + 8])
+                    q += 1
+        else:
+            value = products(zt, chunk, 0, columns)
+            acc[chunk] = value.reshape(acc.shape[1:])
+        start_reduce(chunk, 0)
+        stage[chunk] = 0
+
+    make_forms(3)
+    begin(3)
+    make_forms(2)
+    begin(2)
+    make_forms(1)
+    make_forms(0)
+    begin(GRAM)
+    begin(1)
+    advance(3)
+    begin(0)
+    for chunk in (2, GRAM, 3, 1, 0):
+        advance(chunk)
+    while stage[GRAM] < 2 * BITS:
+        for chunk in (3, 2, GRAM, 1, 0):
+            limit = 2 * BITS if chunk in (3, GRAM) else BITS
+            if stage[chunk] < limit:
+                advance(chunk)
+    finish_gram()
+    for b in (2, 1, 0):
+        solve(b)
+        start_spread(b, 0)
+
+    def take(b):
+        high, low = split(xt[b].reshape(columns, 256))
+        xk[0, :, b * 256:(b + 1) * 256] = high
+        xk[1, :, b * 256:(b + 1) * 256] = low
+
+    def update(first, count, last):
+        lanes = slice(first * 256, (first + count) * 256)
+
+        @pl.loop(0, rows // 256)
+        def _(step):
+            part = pl.ds(pl.multiple_of(step * 256, 256), 256)
+            for p in range(2):
+                f_high, f_low = forms[p, 0, part, lanes], forms[p, 1, part, lanes]
+                x_high, x_low = xk[0, :, lanes], xk[1, :, lanes]
+                z[p, part, :] = z[p, part, :] - (
+                    dot_lanes(f_high, x_high) + dot_lanes(f_high, x_low) + dot_lanes(f_low, x_high))
+                if last:
+                    pltpu.make_async_copy(
+                        z.at[p, part, :], out_hbm.at[p, part, :], out_sem.at[p, step]).start()
+
+    for _ in range(BITS - 1):
+        for b in (2, 1, 0):
+            advance(b)
+    advance(2)
+    take(3)
+    take(2)
+    update(2, 2, False)
+    advance(1)
+    advance(0)
+    take(1)
+    take(0)
+    update(0, 2, True)
+    for copy in sends:
+        copy.wait_send()
+
+    @pl.loop(0, rows // 256)
+    def _(step):
+        part = pl.ds(pl.multiple_of(step * 256, 256), 256)
+        for p in range(2):
+            pltpu.make_async_copy(z.at[p, part, :], out_hbm.at[p, part, :], out_sem.at[p, step]).wait()
+
+
+def fused_shards(eigenvectors, reflectors, reflector_factors):
+    blocks, _, rows, share = reflectors.shape
+    columns = eigenvectors.shape[2]
+    width = reflector_factors.shape[2]
+    packed = jnp.concatenate([reflectors[:, 0], reflectors[:, 1]], axis=2)
+    turned = jnp.swapaxes(reflector_factors, 2, 3)
+    whole = jnp.stack([turned, jnp.stack([-turned[:, 1], turned[:, 0]], axis=1)], axis=1)
+    whole = whole.reshape(blocks, 2, 2, 2, share, 2, share).transpose(0, 3, 1, 4, 5, 2, 6)
+    whole = whole.reshape(blocks, 2 * width, 2 * width)
+    two = (2,) * BITS
+    owned = columns // 2 ** BITS
+    vmem = pltpu.VMEM
+    dma = pltpu.SemaphoreType.DMA
+    slot_shapes = [vmem((blocks,) + (2,) * (BITS - 1 - s) + (owned, 2 * width), F32) for s in range(BITS)]
+    gslot_shapes = [vmem((2,) * (BITS - 1 - s) + (3, 8, 2 * width), F32) for s in range(BITS)]
+    scratch = [
+        vmem((2, rows, columns), F32),
+        vmem((2, 2, columns, rows), BF16),
+        vmem((blocks, rows, width), F32),
+        vmem((blocks, rows, width), F32),
+        vmem((2, 2, blocks * share, rows), BF16),
+        vmem((2, 2, rows, blocks * 2 * width), BF16),
+        vmem((blocks,) + two + (owned, 2 * width), F32),
+        vmem(two + (3, 8, 2 * width), F32),
+        slot_shapes,
+        gslot_shapes,
+        vmem((blocks,) + two + (owned, 2 * width), F32),
+        vmem(two + (3, 8, 2 * width), F32),
+        vmem(two + (3, 8, 2 * width), F32),
+        vmem((2, columns, blocks * 2 * width), BF16),
+        vmem((6, 2 * width, 2 * width), F32),
+        dma((2,)),
+        dma((blocks,)),
+        dma((2, rows // 256)),
+        dma((blocks + 1,)),
+        dma((blocks + 1,)),
+        dma((blocks + 1, 2 * BITS)),
+        dma((blocks + 1, 2 * BITS)),
+    ]
+    anywhere = pl.BlockSpec(memory_space=pl.ANY)
+    near = pl.BlockSpec(memory_space=pltpu.VMEM)
+    flops = 2 * 2 * 3 * 4 * blocks * width * rows * columns
+    return pl.pallas_call(
+        kernel,
+        out_shape=jax.ShapeDtypeStruct(eigenvectors.shape, F32),
+        in_specs=[anywhere, anywhere, near],
+        out_specs=anywhere,
+        scratch_shapes=scratch,
+        compiler_params=pltpu.CompilerParams(
+            collective_id=0, has_side_effects=True, vmem_limit_bytes=60 * 1024 * 1024),
+        cost_estimate=pl.CostEstimate(flops=flops, bytes_accessed=16 * 1024 * 1024, transcendentals=0),
+    )(eigenvectors, packed, whole)
 
 
 def product(spec, left_side, right_side):
@@ -49,6 +399,7 @@
 
 def solution(mesh):
     placed = (P(None, "row", "col"), P(None, None, "row", "col"), P())
+    fused = mesh.shape["row"] == 2 ** BITS and mesh.shape["col"] == 2
     return jax.shard_map(
-        merged_shards, mesh=mesh, in_specs=placed, out_specs=P(None, "row", "col"), check_vma=False
+        fused_shards if fused else merged_shards, mesh=mesh, in_specs=placed, out_specs=P(None, "row", "col"), check_vma=False
     )

time: 295 us -> 129 us (0.44)
  waiting for transfers between devices: 199 us -> 0 us
  Pallas kernels: 0 us -> 100 us
  matrix products: 44 us -> 0 us
  between operations: 14.2 us -> 0.08 us
  local copies, waits for them, and re-layouts: 27.4 us -> 20.4 us
    unnamed x4 -> x0, waiting for transfers between devices: 134 us -> none
    pallas_call x0 -> x1, Pallas kernels: none -> 100 us  [fused_shards(): pl.pallas_call(kernel, out_shape=jax.ShapeDtypeStruct(eigenvectors.shape,...]
    all_gather x2 -> x0, waiting for transfers between devices: 64.8 us -> none  [the longest x1 49.9 us: merged_shards(): lax.all_gather(jnp.concatenate(results, axis=2), 'row', axis=1, tiled=True)]
    dot_general x60 -> x0, matrix products: 44 us -> none  [product(): return jnp.einsum(spec, left_side, right_side, precision=lax.Precision.HIGH)]
    sub x1 -> x0, local copies, waits for them, and re-layouts: 5.88 us -> none  [merged_shards(): return eigenvectors - complex_rows('nk,mk->nm', flat, result)]
    slice x5 -> x1, local copies, waits for them, and re-layouts: 6.73 us -> 3.4 us  [fused_shards(): packed = jnp.concatenate([reflectors[:, 0], reflectors[:, 1]], axis=2)]
    sub x4 -> x0, other arithmetic: 3.09 us -> none  [the longest x1 2.96 us: merged_shards(): return eigenvectors - complex_rows('nk,mk->nm', flat, result)]
    unnamed x27 -> x5, local copies, waits for them, and re-layouts: 10.3 us -> 10.3 us
  transfers between devices with their start and end apart: 3 -> 0, of which waited for: 3 -> 0; matrix products, arithmetic and copies ran while one was open for 5% -> 0% of each run, Pallas kernels for 0% -> 0%
where the time goes in v2:
time: 129 us; the launch traced here: 128 us
  Pallas kernels  100 us (78%)
  local copies, waits for them, and re-layouts  20.4 us (16%)
  other arithmetic  7.57 us (6%)
    pallas_call x1, Pallas kernels, fused_shards(): pl.pallas_call(kernel, out_shape=jax.ShapeDtypeStruct(eigenvectors.shape,...  100 us
    unnamed x5, local copies, waits for them, and re-layouts  10.3 us
    another operation x4, local copies, waits for them, and re-layouts, fused_shards(): jnp.stack([turned, jnp.stack([-turned[:, 1], turned[:, 0]], axis=1)], axi...  4.01 us
    concatenate x1, other arithmetic, fused_shards(): packed = jnp.concatenate([reflectors[:, 0], reflectors[:, 1]], axis=2)  3.99 us
    slice x1, local copies, waits for them, and re-layouts, fused_shards(): packed = jnp.concatenate([reflectors[:, 0], reflectors[:, 1]], axis=2)  3.4 us
    reshape x1, local copies, waits for them, and re-layouts, fused_shards(): whole = whole.reshape(blocks, 2 * width, 2 * width)  2.66 us

profile of v2, /device:TPU:0, one launch (start us, length us, event | category | flops | bytes accessed | tf_op | source)
XLA Modules:
  0.0 128.4 jit_solution(9095297120907074716)
XLA Ops:
  0.0 1.1 slice_negate_fusion
  1.1 0.0 copy-start
  1.1 0.6 stack.15
  1.7 0.9 copy.7
  2.7 0.0 copy-done
  2.7 0.6 stack.13
  3.3 1.9 %copy.6 = f32[4,1,2,2,64,2,64]{6,2,5,4,1,3,0:T(2,128)} copy(f32[4,1,2,2,64,2,64]{4,3,6,5,2,0,1:T(2,128)S(1)} %stack.13) | data formatting | bytes 1048576 | tf_op jit(solution)/shard_map/stack | solution.py:309
  5.2 2.5 %maximum_bitcast_fusion = f32[4,2,2,64,2,2,64]{6,5,4,3,2,1,0:T(2,128)S(1)} fusion(f32[4,1,2,2,64,2,64]{6,2,5,4,1,3,0:T(2,128)S(1)} %copy.7, f32[4,1,2,2,64,2,64]{6,2,5,4,1,3,0:T(2,128)} %copy.6), kind=kLoop, calls=%fused_computation.1 | loop fusion | flops 262144 | bytes 2097152 | tf_op jit(solution)/shard_map/transpose | solution.py:310
  7.7 2.7 %reshape.8.factors = f32[4,256,256]{2,1,0:T(8,128)} reshape(f32[4,2,2,64,2,2,64]{6,5,4,3,2,1,0:T(2,128)S(1)} %maximum_bitcast_fusion) | data formatting | bytes 2097152 | tf_op jit(solution)/shard_map/reshape | solution.py:311
  10.3 3.4 %fusion = (f32[4,1,1280,64]{2,3,1,0:T(8,128)}, f32[4,1,1280,64]{2,3,1,0:T(8,128)}) fusion(f32[4,2,1280,64]{2,3,1,0:T(8,128)} %param.4), kind=kLoop, calls=%fused_computation.4 | loop fusion | bytes 5242880 | tf_op jit(solution)/shard_map/slice | solution.py:307
  13.7 1.9 %copy.8 = f32[4,1,1280,64]{3,2,0,1:T(8,128)S(1)} copy(f32[4,1,1280,64]{2,3,1,0:T(8,128)} %get-tuple-element.5) | data formatting | bytes 2621440
  15.6 3.0 %copy.9 = f32[4,1,1280,64]{3,2,0,1:T(8,128)} copy(f32[4,1,1280,64]{2,3,1,0:T(8,128)} %get-tuple-element.6) | data formatting | bytes 2621440
  18.6 4.0 %pad_maximum_fusion.v_hbm = f32[4,1280,128]{2,1,0:T(8,128)} fusion(f32[4,1280,64]{2,1,0:T(8,128)} %bitcast.14, f32[4,1280,64]{2,1,0:T(8,128)S(1)} %bitcast.13), kind=kLoop, calls=%fused_computation | loop fusion | flops 655360 | bytes 5242880 | tf_op jit(solution)/shard_map/concatenate | solution.py:307
  22.6 100.4 %shard_map.37 = f32[2,1280,512]{2,1,0:T(8,128)} custom-call(f32[2,1280,512]{2,1,0:T(8,128)} %z_hbm.1, f32[4,1280,128]{2,1,0:T(8,128)} %pad_maximum_fusion.v_hbm, f32[4,256,256]{2,1,0:T(8,128)} %reshape.8.factors), custom_call_target="tpu_custom_call" | custom-call | flops 16106127360 | bytes 16777216 | tf_op jit(solution)/shard_map/pallas_call | solution.py:345
  123.0 5.4 %copy.11 = f32[2,1280,512]{2,1,0:T(8,128)} copy(f32[2,1280,512]{2,1,0:T(8,128)} %shard_map.37) | data formatting | bytes 10485760
  (1 shorter events, 0.0 us)
Async XLA Ops:
  1.1 1.6 %copy-start = (f32[4,2,128,128]{3,2,1,0:T(8,128)S(1)}, f32[4,2,128,128]{3,2,1,0:T(8,128)}, u32[]{:S(2)}) copy-start(f32[4,2,128,128]{3,2,1,0:T(8,128)} %param.5) | copy-start | bytes 1572868

commit v3 on v2

--- a/solution.py
+++ b/solution.py
@@ -26,11 +26,11 @@
 
 
 def kernel(z_hbm, v_hbm, factors, out_hbm, z, zt, w_own, w_other, vt, forms, acc, gacc,
-           slots, gslots, xt, gx, gother, xk, gram, z_sem, v_sem, out_sem, pair_send, pair_recv,
+           slots, gslots, xt, gx, gother, xk, gram, fact, z_sem, v_sem, out_sem, pair_send, pair_recv,
            row_send, row_recv):
     rows, columns = z.shape[1], z.shape[2]
     blocks = w_own.shape[0]
-    share = w_own.shape[2] // 2
+    share = w_own.shape[1] // 2
     row, col = lax.axis_index("row"), lax.axis_index("col")
     mine = [lax.rem(row // (1 << bit), 2) for bit in range(BITS)]
     partner = [row + (1 << bit) * (1 - 2 * mine[bit]) for bit in range(BITS)]
@@ -69,7 +69,7 @@
     def _(step):
         part = pl.ds(pl.multiple_of(step * 128, 128), 128)
         for b in range(blocks):
-            high, low = split(w_own[b, part, :].T)
+            high, low = split(w_own[b, :, part])
             for p in range(2):
                 vt[0, p, b * share:(b + 1) * share, part] = high[p * share:(p + 1) * share]
                 vt[1, p, b * share:(b + 1) * share, part] = low[p * share:(p + 1) * share]
@@ -88,14 +88,28 @@
     lane = lax.broadcasted_iota(jnp.int32, (1, 128), 1)
     sign = jnp.where(lane < share, 1.0, -1.0).astype(F32)
 
+    for b in range(blocks):
+        real, imag = factors[b, 0], factors[b, 1]
+        real_turned, imag_turned = pltpu.roll(real, share, 1), pltpu.roll(imag, share, 1)
+        first = lane < share
+        parts = (
+            (jnp.where(first, real, -imag_turned), jnp.where(first, real_turned, -imag)),
+            (jnp.where(first, imag, real_turned), jnp.where(first, imag_turned, real)),
+        )
+        for h in range(2):
+            for p in range(2):
+                base = h * 2 * share + p * share
+                for k in range(2):
+                    fact[b, base:base + share, k * 128:(k + 1) * 128] = parts[p][k][h * share:(h + 1) * share]
+
     def make_forms(b):
         v_copies[b].wait_recv()
 
         @pl.loop(0, rows // 256)
         def _(step):
             part = pl.ds(pl.multiple_of(step * 256, 256), 256)
-            own, other = w_own[b, part, :], w_other[b, part, :]
-            halves = (jnp.where(col == 0, own, other), jnp.where(col == 0, other, own))
+            own, other = w_own[b, :, part], w_other[b, :, part]
+            halves = (jnp.where(col == 0, own, other).T, jnp.where(col == 0, other, own).T)
             for h in range(2):
                 lanes = slice(b * 256 + h * 128, b * 256 + h * 128 + 128)
                 for form, value in ((0, halves[h] * sign), (1, pltpu.roll(halves[h], share, 1))):
@@ -190,8 +204,9 @@
         for c in range(b + 1, blocks):
             high, low = split(gram[start + c - b - 1])
             sums = sums - dot3(solved[c], high, low)
-        high, low = split(factors[b])
-        solved[b] = dot3(sums, high, low)
+        s_high, s_low = split(sums)
+        high, low = split(fact[b])
+        solved[b] = dot_lanes(s_high, high) + dot_lanes(s_high, low) + dot_lanes(s_low, high)
         own_part(xt, (b,))[...] = solved[b]
 
     stage = {}
@@ -304,11 +319,7 @@
     blocks, _, rows, share = reflectors.shape
     columns = eigenvectors.shape[2]
     width = reflector_factors.shape[2]
-    packed = jnp.concatenate([reflectors[:, 0], reflectors[:, 1]], axis=2)
-    turned = jnp.swapaxes(reflector_factors, 2, 3)
-    whole = jnp.stack([turned, jnp.stack([-turned[:, 1], turned[:, 0]], axis=1)], axis=1)
-    whole = whole.reshape(blocks, 2, 2, 2, share, 2, share).transpose(0, 3, 1, 4, 5, 2, 6)
-    whole = whole.reshape(blocks, 2 * width, 2 * width)
+    packed = jnp.swapaxes(reflectors, 2, 3).reshape(blocks, 2 * share, rows)
     two = (2,) * BITS
     owned = columns // 2 ** BITS
     vmem = pltpu.VMEM
@@ -318,8 +329,8 @@
     scratch = [
         vmem((2, rows, columns), F32),
         vmem((2, 2, columns, rows), BF16),
-        vmem((blocks, rows, width), F32),
-        vmem((blocks, rows, width), F32),
+        vmem((blocks, width, rows), F32),
+        vmem((blocks, width, rows), F32),
         vmem((2, 2, blocks * share, rows), BF16),
         vmem((2, 2, rows, blocks * 2 * width), BF16),
         vmem((blocks,) + two + (owned, 2 * width), F32),
@@ -331,6 +342,7 @@
         vmem(two + (3, 8, 2 * width), F32),
         vmem((2, columns, blocks * 2 * width), BF16),
         vmem((6, 2 * width, 2 * width), F32),
+        vmem((blocks, 2 * width, 2 * width), F32),
         dma((2,)),
         dma((blocks,)),
         dma((2, rows // 256)),
@@ -351,7 +363,7 @@
         compiler_params=pltpu.CompilerParams(
             collective_id=0, has_side_effects=True, vmem_limit_bytes=60 * 1024 * 1024),
         cost_estimate=pl.CostEstimate(flops=flops, bytes_accessed=16 * 1024 * 1024, transcendentals=0),
-    )(eigenvectors, packed, whole)
+    )(eigenvectors, packed, reflector_factors)
 
 
 def product(spec, left_side, right_side):

time: 129 us -> 107 us (0.83)
  local copies, waits for them, and re-layouts: 20.4 us -> 5.42 us
  other arithmetic: 7.57 us -> 0 us
  Pallas kernels: 100 us -> 102 us
    unnamed x5 -> x1, local copies, waits for them, and re-layouts: 10.3 us -> 5.42 us
    another operation x4 -> x0, local copies, waits for them, and re-layouts: 4.01 us -> none  [fused_shards(): jnp.stack([turned, jnp.stack([-turned[:, 1], turned[:, 0]], axis=1)], axi...]
    concatenate x1 -> x0, other arithmetic: 3.99 us -> none  [fused_shards(): packed = jnp.concatenate([reflectors[:, 0], reflectors[:, 1]], axis=2)]
    slice x1 -> x0, local copies, waits for them, and re-layouts: 3.4 us -> none  [fused_shards(): packed = jnp.concatenate([reflectors[:, 0], reflectors[:, 1]], axis=2)]
    reshape x1 -> x0, local copies, waits for them, and re-layouts: 2.66 us -> none  [fused_shards(): whole = whole.reshape(blocks, 2 * width, 2 * width)]
    transpose x1 -> x0, other arithmetic: 2.48 us -> none  [fused_shards(): whole.reshape(blocks, 2, 2, 2, share, 2, share)]
where the time goes in v3:
time: 107 us
  Pallas kernels  102 us (95%)
  local copies, waits for them, and re-layouts  5.42 us (5%)
    pallas_call x1, Pallas kernels, fused_shards(): pl.pallas_call(kernel, out_shape=jax.ShapeDtypeStruct(eigenvectors.shape,...  102 us
    unnamed x1, local copies, waits for them, and re-layouts  5.42 us

profile of v3, /device:TPU:0, one launch (start us, length us, event | category | flops | bytes accessed | tf_op | source)
XLA Modules:
  0.0 107.1 jit_solution(17168510765601440083)
XLA Ops:
  0.0 101.6 %shard_map.37 = f32[2,1280,512]{2,1,0:T(8,128)} custom-call(f32[2,1280,512]{2,1,0:T(8,128)} %z_hbm.1, f32[4,128,1280]{2,1,0:T(8,128)} %bitcast.3, f32[4,2,128,128]{3,2,1,0:T(8,128)} %factors.1), custom_call_target="tpu_custom_call" | custom-call | flops 16106127360 | bytes 16777216 | tf_op jit(solution)/shard_map/pallas_call | solution.py:357
  101.6 5.4 %copy.5 = f32[2,1280,512]{2,1,0:T(8,128)} copy(f32[2,1280,512]{2,1,0:T(8,128)} %shard_map.37) | data formatting | bytes 10485760
